TPU v7x, 32 devices: a whole 2x2x4 slice. The times are simulated.
32 devices in a mesh: row: 8 (over z, y), col: 4 (over x, core).
Axes of the slice: x: 2, y: 2, z: 4, core: 2. Of those that a mesh axis runs over, the one named last changes fastest.
Arguments:
- a_blocks: float32 [128, 8, 125, 125], P('row', 'col'), may hold values from -0.1875 to 0.1875
- a_pattern: int32 [128, 8], P('row', 'col'), may hold values 0 or 1
- row_owner: int32 [128], replicated, may hold values from 0 to 127, as said below
- prolong: float32 [8, 24, 125, 125], P('row', 'col'), may hold values from -6 to 6
- p_pattern: int32 [8, 24], P('row', 'col'), may hold values 0 or 1
- prolong_slab: float32 [128, 8, 125, 125], P('row'), may hold values from -0.0625 to 0.0625
Outputs:
- coarse: float32 [8, 24, 125, 125], P('row', 'col')
Inputs may be any that keep to these rules, and one draw needn't show every extreme that they name: row_owner is a permutation; the 16 element-order rows e with e // 16 equal go to at most 2 positions p of any one value p // 16, and exactly 2 for each value they reach.
All inputs are finite; a program needn't handle non-finite values. No bound on the sum of `a_pattern` or of `p_pattern` on one device may be relied on, other than what follows from the above.
Results may differ from a plain program's by a relative error of at most 0.0001.
Values sent between devices are 32-bit elements; how exact they have to be, the bound alone decides.
A program may use at most 128 MiB of HBM per device.

v0:
```python
import jax
import jax.numpy as jnp
from jax import lax
from jax.sharding import PartitionSpec as P

CAP = 2


def ranks_of(targets):
    width = targets.shape[-1]
    same = targets[..., :, None] == targets[..., None, :]
    lower = jnp.arange(width)[:, None] > jnp.arange(width)[None, :]
    return jnp.sum(jnp.where(same & lower, 1, 0), axis=-1).astype(jnp.int32)


def pick(rows, at):
    return jnp.stack(
        [lax.dynamic_index_in_dim(rows, at[i], 0, keepdims=False) for i in range(at.shape[0])]
    )


def shards(a_blocks, a_pattern, row_owner, prolong, p_pattern, prolong_slab):
    width = a_blocks.shape[0]
    count = lax.axis_size("row")
    me = lax.axis_index("row")
    masked = a_blocks * a_pattern.astype(jnp.float32)[:, :, None, None]
    p_masked = prolong * p_pattern.astype(jnp.float32)[:, :, None, None]
    p_full = lax.all_gather(p_masked, "row", axis=0, tiled=True)
    table = row_owner.reshape(count, width)
    ranks = ranks_of(table // width)
    targets = lax.dynamic_index_in_dim(table, me, 0, keepdims=False) // width
    mine = lax.dynamic_index_in_dim(ranks, me, 0, keepdims=False)
    slot = targets * CAP + mine
    hit = slot[None, :] == jnp.arange(count * CAP, dtype=jnp.int32)[:, None]
    order = jnp.sum(jnp.where(hit, jnp.arange(width, dtype=jnp.int32)[None, :], 0), axis=1)
    packed = pick(masked, order)
    packed = packed.reshape((count, CAP) + masked.shape[1:])
    received = lax.all_to_all(packed, "row", split_axis=0, concat_axis=0, tiled=True)
    received = received.reshape((count * CAP,) + masked.shape[1:])
    wanted = table[None] == (me * width + jnp.arange(width, dtype=jnp.int32))[:, None, None]
    source = jnp.arange(count, dtype=jnp.int32)[:, None] * CAP + ranks
    where = jnp.sum(jnp.where(wanted, source[None], 0), axis=(1, 2))
    grid_a = pick(received, where)
    part = jnp.einsum(
        "maxy,mkxz->akyz",
        prolong_slab,
        grid_a,
        precision=lax.Precision.HIGH,
        preferred_element_type=jnp.float32,
    )
    mine = lax.psum_scatter(part, "row", scatter_dimension=0, tiled=True)
    mid = lax.all_gather(mine, "col", axis=1, tiled=True)
    return jnp.einsum(
        "akyx,knxz->anyz",
        mid,
        p_full,
        precision=lax.Precision.HIGH,
        preferred_element_type=jnp.float32,
    )


def solution(mesh):
    in_specs = (
        P("row", "col", None, None),
        P("row", "col"),
        P(),
        P("row", "col", None, None),
        P("row", "col"),
        P("row", None, None, None),
    )
    out_specs = P("row", "col", None, None)
    return jax.shard_map(shards, mesh=mesh, in_specs=in_specs, out_specs=out_specs, check_vma=False)
```

profile of v0, /device:TPU:0, one launch (start us, length us, event | category | flops | bytes accessed | tf_op | source)
XLA Modules:
  0.0 269.7 jit_solution(4542487792375120371)
XLA Ops:
  6.5 0.7 reshape.110
  7.7 0.7 fusion.16
  28.4 0.7 convert_element_type.7
  29.8 2.3 broadcast_multiply_fusion
  32.1 0.7 dynamic-slice_dynamic-update-slice_fusion.31
  33.4 0.7 dynamic-slice_dynamic-update-slice_fusion.30
  34.6 0.7 dynamic-slice_dynamic-update-slice_fusion.29
  35.9 0.7 dynamic-slice_dynamic-update-slice_fusion.28
  38.5 0.7 dynamic-slice_dynamic-update-slice_fusion.26
  39.8 0.7 dynamic-slice_dynamic-update-slice_fusion.25
  41.2 0.7 dynamic-slice_dynamic-update-slice_fusion.24
  42.4 0.7 dynamic-slice_dynamic-update-slice_fusion.23
  43.8 0.7 dynamic-slice_dynamic-update-slice_fusion.22
  45.0 0.7 dynamic-slice_dynamic-update-slice_fusion.21
  46.3 0.7 dynamic-slice_dynamic-update-slice_fusion.20
  47.6 0.7 dynamic-slice_dynamic-update-slice_fusion.19
  48.9 0.7 dynamic-slice_dynamic-update-slice_fusion.18
  50.2 0.7 dynamic-slice_dynamic-update-slice_fusion.17
  51.5 0.7 dynamic-slice_dynamic-update-slice_fusion.16
  52.2 7.3 %all-to-all-start = ((f32[8,2,2,125,125]{4,2,3,1,0:T(2,128)}), f32[8,2,2,125,125]{4,2,3,1,0:T(2,128)}, u32[]{:S(2)}, u32[]{:S(2)}) async-start(f32[8,2,2,125,125]{4,2,3,1,0:T(2,128)} %bitcast.84), calls=%async_computation | async-start | bytes 4096000 | tf_op jit(solution)/shard_map/all_to_all | solution.py:38
  60.0 0.7 fusion.15
  90.4 16.4 %all-to-all-done = f32[8,2,2,125,125]{4,2,3,1,0:T(2,128)} async-done(((f32[8,2,2,125,125]{4,2,3,1,0:T(2,128)}), f32[8,2,2,125,125]{4,2,3,1,0:T(2,128)}, u32[]{:S(2)}, u32[]{:S(2)}) %all-to-all-start) | async-done | bytes 2000032 | tf_op jit(solution)/shard_map/all_to_all | solution.py:38
  106.7 2.8 %copy.31 = f32[8,2,2,125,125]{3,4,1,0,2:T(8,128)S(1)} copy(f32[8,2,2,125,125]{4,2,3,1,0:T(2,128)} %all-to-all-done) | data formatting | bytes 4000000 | tf_op jit(solution)/shard_map/all_to_all | solution.py:38
  110.0 8.5 %fusion.4 = f32[8,2,125,125]{2,3,0,1:T(8,128)S(1)} fusion(f32[16,8,125,125]{3,1,2,0:T(8,128)} %param.11, f32[16,2,125,125]{2,3,0,1:T(8,128)S(1)} %dynamic-slice_dynamic-update-slice_fusion), kind=kOutput, calls=%fused_computation.4 | convolution fusion | flops 3000000000 | bytes 11000000 | tf_op jit(solution)/shard_map/maxy,mkxz->akyz/dot_general | solution.py:44
  118.5 1.4 copy.33
  120.4 0.8 broadcast_multiply_fusion.1
  121.9 75.0 %all-reduce.3.cloned.1.call-done = f32[8,2,125,125]{3,1,2,0:T(2,128)} async-done(((f32[8,2,125,125]{3,1,2,0:T(2,128)}), f32[8,2,125,125]{3,1,2,0:T(2,128)}) %all-reduce.3.cloned.1.call-update) | async-done | bytes 1000016
  196.9 1.6 constant_dynamic-slice_fusion.2
  198.6 7.1 %all_gather.7 = f32[1,8,125,125]{3,0,2,1:T(1,128)S(1)} all-gather(f32[1,2,125,125]{3,0,2,1:T(1,128)S(1)} %copy.34), channel_id=1, replica_groups=mesh['row'=8,'col'=4] {'col'}, dimensions={1}, use_global_device_ids=true | all-gather | bytes 625000 | tf_op jit(solution)/shard_map/all_gather | solution.py:52
  205.7 52.9 %all-gather.2.cloned.1.call-done = f32[8,6,125,125]{2,3,0,1:T(8,128)} async-done(((f32[1,6,125,125]{2,3,0,1:T(8,128)}), f32[8,6,125,125]{2,3,0,1:T(8,128)}) %all-gather.2.cloned.1.call-update) | async-done | bytes 3000016 | tf_op jit(solution)/shard_map/all_gather | solution.py:28
  258.6 3.3 %convolution_bitcast_fusion = f32[1,6,125,125]{2,3,1,0:T(8,128)S(1)} fusion(f32[8,6,125,125]{2,3,0,1:T(8,128)} %all-gather.2.cloned.1.call-done, f32[1,8,125,125]{3,0,2,1:T(1,128)S(1)} %all_gather.7), kind=kOutput, calls=%fused_computation.5 | convolution fusion | flops 562499968 | bytes 3875000 | tf_op jit(solution)/shard_map/akyx,knxz->anyz/dot_general | solution.py:53
  261.9 1.0 copy.37
  (41 shorter events, 3.2 us)
Async XLA Ops:
  52.2 54.6 %all-to-all-start = ((f32[8,2,2,125,125]{4,2,3,1,0:T(2,128)}), f32[8,2,2,125,125]{4,2,3,1,0:T(2,128)}, u32[]{:S(2)}, u32[]{:S(2)}) async-start(f32[8,2,2,125,125]{4,2,3,1,0:T(2,128)} %bitcast.84), calls=%async_computation | async-start | bytes 4096000 | tf_op jit(solution)/shard_map/all_to_all | solution.py:38
  59.4 137.5 %all-reduce.3.cloned.1.call-start = ((), (), s32[]{:S(2)}) async-start(), calls=%async_computation.2 | async-start | bytes 2048000
  118.5 1.5 copy-start
  118.5 1.9 copy-start.1
  118.5 2.7 %copy-start.2 = (u32[32]{0:T(128)S(1)}, u32[32]{0:T(128)}, u32[]{:S(2)}) copy-start(u32[32]{0:T(128)} %constant.116) | copy-start | bytes 388
  119.9 138.6 %all-gather.2.cloned.1.call-start = ((), (), s32[]{:S(2)}) async-start(), calls=%async_computation.1 | async-start | bytes 3538944 | tf_op jit(solution)/shard_map/all_gather | solution.py:28
Sparse Core Ops, SparseCore 0:
  120.1 76.7 all-reduce.2
  199.1 59.4 all-gather.1
where the time goes:
time: 271 us; the launch traced here: 270 us
  waiting for transfers between devices  144 us (53%)
  between operations  73.3 us (27%)
  local copies, waits for them, and re-layouts  21.1 us (8%)
  matrix products  11.8 us (4%)
  starting transfers between devices  7.36 us (3%)
  blocking collectives  7.08 us (3%)
  other arithmetic  4.83 us (2%)
    unnamed x3, waiting for transfers between devices  75.1 us
    all_gather x1, waiting for transfers between devices, shards(): p_full = lax.all_gather(p_masked, 'row', axis=0, tiled=True)  52.9 us
    all_to_all x1, waiting for transfers between devices, shards(): lax.all_to_all(packed, 'row', split_axis=0, concat_axis=0, tiled=True)  16.4 us
    unnamed x39, local copies, waits for them, and re-layouts  12.8 us
    dot_general x1, matrix products, shards(): jnp.einsum('maxy,mkxz->akyz', prolong_slab, grid_a, precision=lax.Precisi...  8.49 us
    all_to_all x1, starting transfers between devices, shards(): lax.all_to_all(packed, 'row', split_axis=0, concat_axis=0, tiled=True)  7.28 us
    all_gather x1, blocking collectives, shards(): mid = lax.all_gather(mine, 'col', axis=1, tiled=True)  7.08 us
  transfers between devices with their start and end apart: 3, of which 3 were waited for; matrix products, arithmetic and copies ran while one was open for 2% of the time, Pallas kernels for 0%

commit v1 on v0

--- a/solution.py
+++ b/solution.py
@@ -20,12 +20,40 @@
 
 
 def shards(a_blocks, a_pattern, row_owner, prolong, p_pattern, prolong_slab):
+
+    def start_unit(here_x, x_local):
+        across = "row"
+        state_next = lax.psum(1, across)
+        value_now, mid_arr, arr_next = (state_next, lax.axis_index(across), here_x.shape[0])
+        shelf = []
+        u = 0
+        while u < value_now:
+            shelf.append((u, (u + 1) % value_now))
+            u = u + 1
+        buffer = []
+        u = 0
+        while u < value_now:
+            buffer.append((u, (u - 1) % value_now))
+            u = u + 1
+        everything = value_now // 2
+        current_block = val = here_x
+        r_now = x_local(here_x, mid_arr * arr_next)
+        dev_i = 1
+        while dev_i < everything + 1:
+            current_block = lax.ppermute(current_block, across, shelf)
+            if dev_i < value_now - everything:
+                val = lax.ppermute(val, across, buffer)
+                heard = x_local(val, (mid_arr + dev_i) % value_now * arr_next)
+                r_now = r_now + heard
+            r_now = r_now + x_local(current_block, (mid_arr - dev_i) % value_now * arr_next)
+            dev_i += 1
+        return r_now
+
     width = a_blocks.shape[0]
     count = lax.axis_size("row")
     me = lax.axis_index("row")
     masked = a_blocks * a_pattern.astype(jnp.float32)[:, :, None, None]
     p_masked = prolong * p_pattern.astype(jnp.float32)[:, :, None, None]
-    p_full = lax.all_gather(p_masked, "row", axis=0, tiled=True)
     table = row_owner.reshape(count, width)
     ranks = ranks_of(table // width)
     targets = lax.dynamic_index_in_dim(table, me, 0, keepdims=False) // width
@@ -50,12 +78,15 @@
     )
     mine = lax.psum_scatter(part, "row", scatter_dimension=0, tiled=True)
     mid = lax.all_gather(mine, "col", axis=1, tiled=True)
-    return jnp.einsum(
-        "akyx,knxz->anyz",
-        mid,
-        p_full,
-        precision=lax.Precision.HIGH,
-        preferred_element_type=jnp.float32,
+    return start_unit(
+        p_masked,
+        lambda part_2, start: jnp.einsum(
+            "akyx,knxz->anyz",
+            lax.dynamic_slice_in_dim(mid, start, part_2.shape[0], axis=1),
+            part_2,
+            precision=lax.Precision.HIGH,
+            preferred_element_type=jnp.float32,
+        ),
     )
 
 

time: 271 us -> 248 us (0.915)
  waiting for transfers between devices: 144 us -> 105 us
  starting transfers between devices: 7.36 us -> 24.8 us
    all_gather x1 -> x0, waiting for transfers between devices: 52.9 us -> none  [shards(): p_full = lax.all_gather(p_masked, 'row', axis=0, tiled=True)]
    ppermute x0 -> x7, waiting for transfers between devices: none -> 46.4 us  [the longest x4 26.6 us: start_unit(): current_block = lax.ppermute(current_block, across, shelf)]
    unnamed x3 -> x2, waiting for transfers between devices: 75.1 us -> 44.5 us
    ppermute x0 -> x7, starting transfers between devices: none -> 17.4 us  [the longest x4 14.6 us: start_unit(): current_block = lax.ppermute(current_block, across, shelf)]
  transfers between devices with their start and end apart: 3 -> 9, of which waited for: 3 -> 6; matrix products, arithmetic and copies ran while one was open for 2% -> 8% of each run, Pallas kernels for 0% -> 0%
where the time goes in v1:
time: 248 us; the launch traced here: 247 us
  waiting for transfers between devices  105 us (42%)
  between operations  73.6 us (30%)
  starting transfers between devices  24.8 us (10%)
  local copies, waits for them, and re-layouts  21.1 us (9%)
  matrix products  11.1 us (4%)
  blocking collectives  7.08 us (3%)
  other arithmetic  4.08 us (2%)
    unnamed x2, waiting for transfers between devices  44.5 us
    ppermute x4, waiting for transfers between devices, start_unit(): current_block = lax.ppermute(current_block, across, shelf)  26.6 us
    ppermute x3, waiting for transfers between devices, start_unit(): val = lax.ppermute(val, across, buffer)  19.8 us
    ppermute x4, starting transfers between devices, start_unit(): current_block = lax.ppermute(current_block, across, shelf)  14.6 us
    all_to_all x1, waiting for transfers between devices, shards(): lax.all_to_all(packed, 'row', split_axis=0, concat_axis=0, tiled=True)  13.7 us
    unnamed x39, local copies, waits for them, and re-layouts  12.7 us
    dot_general x1, matrix products, shards(): jnp.einsum('maxy,mkxz->akyz', prolong_slab, grid_a, precision=lax.Precisi...  8.49 us
    all_to_all x1, starting transfers between devices, shards(): lax.all_to_all(packed, 'row', split_axis=0, concat_axis=0, tiled=True)  7.41 us
  transfers between devices with their start and end apart: 9, of which 6 were waited for; matrix products, arithmetic and copies ran while one was open for 8% of the time, Pallas kernels for 0%

profile of v1, /device:TPU:0, one launch (start us, length us, event | category | flops | bytes accessed | tf_op | source)
XLA Modules:
  0.0 246.5 jit_solution(9653345517566798977)
XLA Ops:
  6.5 0.7 reshape.166
  7.7 0.7 fusion.28
  28.5 0.7 convert_element_type.7
  29.8 2.3 broadcast_multiply_fusion
  32.2 0.7 dynamic-slice_dynamic-update-slice_fusion.31
  34.9 0.7 dynamic-slice_dynamic-update-slice_fusion.29
  37.4 0.7 dynamic-slice_dynamic-update-slice_fusion.27
  38.7 0.7 dynamic-slice_dynamic-update-slice_fusion.26
  40.0 0.7 dynamic-slice_dynamic-update-slice_fusion.25
  41.2 0.7 dynamic-slice_dynamic-update-slice_fusion.24
  43.8 0.7 dynamic-slice_dynamic-update-slice_fusion.22
  45.1 0.7 dynamic-slice_dynamic-update-slice_fusion.21
  51.7 0.7 dynamic-slice_dynamic-update-slice_fusion.16
  52.3 7.4 %all-to-all-start = ((f32[8,2,2,125,125]{4,2,3,1,0:T(2,128)}), f32[8,2,2,125,125]{4,2,3,1,0:T(2,128)}, u32[]{:S(2)}, u32[]{:S(2)}) async-start(f32[8,2,2,125,125]{4,2,3,1,0:T(2,128)} %bitcast.140), calls=%async_computation | async-start | bytes 4096000 | tf_op jit(solution)/shard_map/all_to_all | solution.py:66
  60.3 2.0 collective-permute-start.1
  62.9 0.7 fusion.27
  93.3 13.7 %all-to-all-done = f32[8,2,2,125,125]{4,2,3,1,0:T(2,128)} async-done(((f32[8,2,2,125,125]{4,2,3,1,0:T(2,128)}), f32[8,2,2,125,125]{4,2,3,1,0:T(2,128)}, u32[]{:S(2)}, u32[]{:S(2)}) %all-to-all-start) | async-done | bytes 2000032 | tf_op jit(solution)/shard_map/all_to_all | solution.py:66
  107.1 2.8 %copy.42 = f32[8,2,2,125,125]{3,4,1,0,2:T(8,128)S(1)} copy(f32[8,2,2,125,125]{4,2,3,1,0:T(2,128)} %all-to-all-done) | data formatting | bytes 4000000 | tf_op jit(solution)/shard_map/all_to_all | solution.py:66
  110.3 8.5 %fusion.4 = f32[8,2,125,125]{2,3,0,1:T(8,128)S(1)} fusion(f32[16,8,125,125]{3,1,2,0:T(8,128)} %param.11, f32[16,2,125,125]{2,3,0,1:T(8,128)S(1)} %dynamic-slice_dynamic-update-slice_fusion), kind=kOutput, calls=%fused_computation.4 | convolution fusion | flops 3000000000 | bytes 11000000 | tf_op jit(solution)/shard_map/maxy,mkxz->akyz/dot_general | solution.py:72
  118.8 1.3 copy.44
  120.2 2.5 %collective-permute-start = (f32[1,6,125,125]{2,3,1,0:T(8,128)S(1)}, f32[1,6,125,125]{2,3,1,0:T(8,128)S(1)}, u32[]{:S(2)}, u32[]{:S(2)}) collective-permute-start(f32[1,6,125,125]{2,3,1,0:T(8,128)S(1)} %broadcast_multiply_fusion.1), channel_id=1, source_target_pairs={{0,28},{4,0},{8,4},{12,8},{16,12},{20,16},{24,20},{28,24},{1,29},{... | collective-permute-start | bytes 1125008 | tf_op jit(solution)/shard_map/ppermute | solution.py:45
  122.7 7.5 %collective-permute-start.3 = (f32[1,6,125,125]{2,3,1,0:T(8,128)S(1)}, f32[1,6,125,125]{2,3,1,0:T(8,128)S(1)}, u32[]{:S(2)}, u32[]{:S(2)}) collective-permute-start(f32[1,6,125,125]{2,3,1,0:T(8,128)S(1)} %collective-permute-done.1), channel_id=1, source_target_pairs={{0,4},{4,8},{8,12},{12,16},{16,20},{20,24},{24,28},{28,0},{1,5},{5... | collective-permute-start | bytes 1125008 | tf_op jit(solution)/shard_map/ppermute | solution.py:43
  130.2 18.0 %collective-permute-done = f32[1,6,125,125]{2,3,1,0:T(8,128)S(1)} collective-permute-done((f32[1,6,125,125]{2,3,1,0:T(8,128)S(1)}, f32[1,6,125,125]{2,3,1,0:T(8,128)S(1)}, u32[]{:S(2)}, u32[]{:S(2)}) %collective-permute-start) | collective-permute-done | bytes 375032 | tf_op jit(solution)/shard_map/ppermute | solution.py:45
  148.2 10.3 %collective-permute-done.3 = f32[1,6,125,125]{2,3,1,0:T(8,128)S(1)} collective-permute-done((f32[1,6,125,125]{2,3,1,0:T(8,128)S(1)}, f32[1,6,125,125]{2,3,1,0:T(8,128)S(1)}, u32[]{:S(2)}, u32[]{:S(2)}) %collective-permute-start.3) | collective-permute-done | bytes 375032 | tf_op jit(solution)/shard_map/ppermute | solution.py:43
  158.5 2.6 %collective-permute-start.5 = (f32[1,6,125,125]{2,3,1,0:T(8,128)S(1)}, f32[1,6,125,125]{2,3,1,0:T(8,128)S(1)}, u32[]{:S(2)}, u32[]{:S(2)}) collective-permute-start(f32[1,6,125,125]{2,3,1,0:T(8,128)S(1)} %collective-permute-done.3), channel_id=1, source_target_pairs={{0,4},{4,8},{8,12},{12,16},{16,20},{20,24},{24,28},{28,0},{1,5},{5... | collective-permute-start | bytes 1125008 | tf_op jit(solution)/shard_map/ppermute | solution.py:43
  161.7 1.9 collective-permute-done.2
  163.8 16.3 %collective-permute-done.5 = f32[1,6,125,125]{2,3,1,0:T(8,128)S(1)} collective-permute-done((f32[1,6,125,125]{2,3,1,0:T(8,128)S(1)}, f32[1,6,125,125]{2,3,1,0:T(8,128)S(1)}, u32[]{:S(2)}, u32[]{:S(2)}) %collective-permute-start.5) | collective-permute-done | bytes 375032 | tf_op jit(solution)/shard_map/ppermute | solution.py:43
  180.1 2.5 %collective-permute-start.6 = (f32[1,6,125,125]{2,3,1,0:T(8,128)S(1)}, f32[1,6,125,125]{2,3,1,0:T(8,128)S(1)}, u32[]{:S(2)}, u32[]{:S(2)}) collective-permute-start(f32[1,6,125,125]{2,3,1,0:T(8,128)S(1)} %collective-permute-done.5), channel_id=1, source_target_pairs={{0,4},{4,8},{8,12},{12,16},{16,20},{20,24},{24,28},{28,0},{1,5},{5... | collective-permute-start | bytes 1125008 | tf_op jit(solution)/shard_map/ppermute | solution.py:43
  182.6 44.5 %all-reduce.3.cloned.1.call-done = f32[8,2,125,125]{3,1,2,0:T(2,128)} async-done(((f32[8,2,125,125]{3,1,2,0:T(2,128)}), f32[8,2,125,125]{3,1,2,0:T(2,128)}) %all-reduce.3.cloned.1.call-update) | async-done | bytes 1000016
  227.1 1.6 constant_dynamic-slice_fusion.10
  228.8 7.1 %all_gather.3 = f32[1,8,125,125]{3,0,2,1:T(1,128)S(1)} all-gather(f32[1,2,125,125]{3,0,2,1:T(1,128)S(1)} %copy.45), channel_id=1, replica_groups=mesh['row'=8,'col'=4] {'col'}, dimensions={1}, use_global_device_ids=true | all-gather | bytes 625000 | tf_op jit(solution)/shard_map/all_gather | solution.py:80
  238.7 1.0 copy.54
  (60 shorter events, 10.1 us)
Async XLA Ops:
  52.3 7.5 %copy-start = (f32[1,6,125,125]{3,0,2,1:T(1,128)S(1)}, f32[1,6,125,125]{3,0,2,1:T(1,128)}, u32[]{:S(2)}) copy-start(f32[1,6,125,125]{3,0,2,1:T(1,128)} %param.9) | copy-start | bytes 1125004
  52.3 7.8 %copy-start.1 = (s32[1,6]{1,0:T(1,128)S(1)}, s32[1,6]{1,0:T(1,128)}, u32[]{:S(2)}) copy-start(s32[1,6]{1,0:T(1,128)} %param.10) | copy-start | bytes 76
  52.3 54.7 %all-to-all-start = ((f32[8,2,2,125,125]{4,2,3,1,0:T(2,128)}), f32[8,2,2,125,125]{4,2,3,1,0:T(2,128)}, u32[]{:S(2)}, u32[]{:S(2)}) async-start(f32[8,2,2,125,125]{4,2,3,1,0:T(2,128)} %bitcast.140), calls=%async_computation | async-start | bytes 4096000 | tf_op jit(solution)/shard_map/all_to_all | solution.py:66
  59.8 167.3 %all-reduce.3.cloned.1.call-start = ((), (), s32[]{:S(2)}) async-start(), calls=%async_computation.1 | async-start | bytes 2048000
  60.3 62.4 %collective-permute-start.1 = (f32[1,6,125,125]{2,3,1,0:T(8,128)S(1)}, f32[1,6,125,125]{2,3,1,0:T(8,128)S(1)}, u32[]{:S(2)}, u32[]{:S(2)}) collective-permute-start(f32[1,6,125,125]{2,3,1,0:T(8,128)S(1)} %broadcast_multiply_fusion.1), channel_id=1, source_target_pairs={{0,4},{4,8},{8,12},{12,16},{16,20},{20,24},{24,28},{28,0},{1,5},{5... | collective-permute-start | bytes 1125008 | tf_op jit(solution)/shard_map/ppermute | solution.py:43
  118.8 42.3 %copy-start.2 = (u32[32]{0:T(128)S(1)}, u32[32]{0:T(128)}, u32[]{:S(2)}) copy-start(u32[32]{0:T(128)} %constant.162) | copy-start | bytes 388
  120.2 28.0 %collective-permute-start = (f32[1,6,125,125]{2,3,1,0:T(8,128)S(1)}, f32[1,6,125,125]{2,3,1,0:T(8,128)S(1)}, u32[]{:S(2)}, u32[]{:S(2)}) collective-permute-start(f32[1,6,125,125]{2,3,1,0:T(8,128)S(1)} %broadcast_multiply_fusion.1), channel_id=1, source_target_pairs={{0,28},{4,0},{8,4},{12,8},{16,12},{20,16},{24,20},{28,24},{1,29},{... | collective-permute-start | bytes 1125008 | tf_op jit(solution)/shard_map/ppermute | solution.py:45
  122.7 35.7 %collective-permute-start.3 = (f32[1,6,125,125]{2,3,1,0:T(8,128)S(1)}, f32[1,6,125,125]{2,3,1,0:T(8,128)S(1)}, u32[]{:S(2)}, u32[]{:S(2)}) collective-permute-start(f32[1,6,125,125]{2,3,1,0:T(8,128)S(1)} %collective-permute-done.1), channel_id=1, source_target_pairs={{0,4},{4,8},{8,12},{12,16},{16,20},{20,24},{24,28},{28,0},{1,5},{5... | collective-permute-start | bytes 1125008 | tf_op jit(solution)/shard_map/ppermute | solution.py:43
  148.2 15.4 %collective-permute-start.2 = (f32[1,6,125,125]{2,3,1,0:T(8,128)S(1)}, f32[1,6,125,125]{2,3,1,0:T(8,128)S(1)}, u32[]{:S(2)}, u32[]{:S(2)}) collective-permute-start(f32[1,6,125,125]{2,3,1,0:T(8,128)S(1)} %collective-permute-done), channel_id=1, source_target_pairs={{0,28},{4,0},{8,4},{12,8},{16,12},{20,16},{24,20},{28,24},{1,29},{... | collective-permute-start | bytes 1125008 | tf_op jit(solution)/shard_map/ppermute | solution.py:45
  158.5 21.6 %collective-permute-start.5 = (f32[1,6,125,125]{2,3,1,0:T(8,128)S(1)}, f32[1,6,125,125]{2,3,1,0:T(8,128)S(1)}, u32[]{:S(2)}, u32[]{:S(2)}) collective-permute-start(f32[1,6,125,125]{2,3,1,0:T(8,128)S(1)} %collective-permute-done.3), channel_id=1, source_target_pairs={{0,4},{4,8},{8,12},{12,16},{16,20},{20,24},{24,28},{28,0},{1,5},{5... | collective-permute-start | bytes 1125008 | tf_op jit(solution)/shard_map/ppermute | solution.py:43
  163.5 74.4 %collective-permute-start.4 = (f32[1,6,125,125]{2,3,1,0:T(8,128)S(1)}, f32[1,6,125,125]{2,3,1,0:T(8,128)S(1)}, u32[]{:S(2)}, u32[]{:S(2)}) collective-permute-start(f32[1,6,125,125]{2,3,1,0:T(8,128)S(1)} %collective-permute-done.2), channel_id=1, source_target_pairs={{0,28},{4,0},{8,4},{12,8},{16,12},{20,16},{24,20},{28,24},{1,29},{... | collective-permute-start | bytes 1125008 | tf_op jit(solution)/shard_map/ppermute | solution.py:45
  180.1 58.2 %collective-permute-start.6 = (f32[1,6,125,125]{2,3,1,0:T(8,128)S(1)}, f32[1,6,125,125]{2,3,1,0:T(8,128)S(1)}, u32[]{:S(2)}, u32[]{:S(2)}) collective-permute-start(f32[1,6,125,125]{2,3,1,0:T(8,128)S(1)} %collective-permute-done.5), channel_id=1, source_target_pairs={{0,4},{4,8},{8,12},{12,16},{16,20},{20,24},{24,28},{28,0},{1,5},{5... | collective-permute-start | bytes 1125008 | tf_op jit(solution)/shard_map/ppermute | solution.py:43
Sparse Core Ops, SparseCore 0:
  120.3 106.7 all-reduce.2
